TPU v7x, 32 devices: a whole 2x2x4 slice. The times are simulated.
32 devices in a mesh: grp: 16 (over z, y, core), rep: 2 (over x).
Axes of the slice: x: 2, y: 2, z: 4, core: 2. Of those that a mesh axis runs over, the one named last changes fastest.
Arguments:
- tokens: bfloat16 [2, 2048, 960], P('rep', 'grp'), may hold values from -6 to 6
- lengths: int32 [2, 4], P('rep'), may hold values from 1 to 1921, 2048 in all within a row
- cotangent: bfloat16 [2, 2048, 960], P('rep', 'grp'), may hold values from -6 to 6
- attn_gain: bfloat16 [960], P('grp'), may hold values from 0.25 to 1.75
- w_query: bfloat16 [960, 960], P('grp'), may hold values from -0.1875 to 0.1875
- key_projection: bfloat16 [960, 320], P('grp'), may hold values from -0.1875 to 0.1875
- value_projection: bfloat16 [960, 320], P('grp'), may hold values from -0.1875 to 0.1875
- w_out: bfloat16 [960, 960], P(None, 'grp'), may hold values from -6 to 6
- ffn_gain: bfloat16 [960], P('grp'), may hold values from 0.25 to 1.75
- w_gate: bfloat16 [960, 2560], P('grp'), may hold values from -0.1875 to 0.1875
- w_up: bfloat16 [960, 2560], P('grp'), may hold values from -0.1875 to 0.1875
- w_down: bfloat16 [2560, 960], P(None, 'grp'), may hold values from -0.125 to 0.125
Outputs:
- out: bfloat16 [2, 2048, 960], P('rep', 'grp')
- d_tokens: float32 [2, 2048, 960], P('rep', 'grp')
- d_attn_gain: float32 [960], P('grp')
- d_w_query: float32 [960, 960], P('grp')
- d_w_key: float32 [960, 320], P('grp')
- d_w_value: float32 [960, 320], P('grp')
- d_w_out: float32 [960, 960], P(None, 'grp')
- d_ffn_gain: float32 [960], P('grp')
- d_w_gate: float32 [960, 2560], P('grp')
- d_w_up: float32 [960, 2560], P('grp')
- d_w_down: float32 [2560, 960], P(None, 'grp')
Inputs may be any that keep to these rules, and one draw needn't show every extreme that they name: `lengths`: each row holds the token counts of 4 documents packed in order into one sequence; they sum to 2048, and the longest holds exactly 1921 tokens.
All inputs are finite; a program needn't handle non-finite values.
Results may differ from a plain program's by a relative error of at most 0.02.
Values may be sent and summed in bfloat16 or wider, within the bound.
A program may use at most 192 MiB of HBM per device.

v0:
```python
import functools
import math

import jax
import jax.numpy as jnp
from jax import lax
from jax.experimental import pallas as pl
from jax.experimental.pallas import tpu as pltpu
from jax.sharding import PartitionSpec as P

QUERY_HEADS = 15
KEY_VALUE_HEADS = 5
HEAD_WIDTH = 64


EPS = 1e-05
THETA = 10000.0
NEG = -1e30


def frequencies(head_size):
    steps = jnp.arange(head_size // 2, dtype=jnp.float32)
    return jnp.exp(steps * (-2.0 * math.log(THETA) / head_size))


def rotary_apply(vectors, cosine_table, sine_table):
    half = vectors.shape[-1] // 2
    first = vectors[..., :half]
    second = vectors[..., half:]
    return jnp.concatenate(
        [first * cosine_table - second * sine_table, second * cosine_table + first * sine_table],
        axis=-1,
    )


def doc_layout(lengths_row, places):
    ends = jnp.cumsum(lengths_row)
    before = ends[None, :] <= places[:, None]
    doc_ids = jnp.sum(before.astype(jnp.int32), axis=1)
    starts = jnp.sum(jnp.where(before, lengths_row[None, :], 0), axis=1)
    return (doc_ids, places - starts)


def norm_back(inputs, inv_root, gain, grad_normed, width):
    scaled = gain * grad_normed
    inner = jnp.sum(inputs * scaled, axis=-1, keepdims=True) / width
    grad_inputs = inv_root * scaled - inputs * inv_root**3 * inner
    grad_gain = jnp.sum(grad_normed * inputs * inv_root, axis=0)
    return (grad_inputs, grad_gain)


MESH = pl.DeviceIdType.MESH


def ring_place(chips):
    me = lax.axis_index("grp")
    core = lax.rem(me, 2)
    chip = me // 2
    column = lax.rem(chip, 2)
    level = chip // 2
    position = level + column * (chips - 1 - 2 * level)
    return me, core, position, 1 - 2 * core


def ring_index(position, core, chips):
    place = lax.rem(position + 2 * chips, chips)
    column = place // (chips // 2)
    level = place + column * (chips - 1 - 2 * place)
    return (2 * level + column) * 2 + core


def greet(devices):
    barrier = pltpu.get_barrier_semaphore()
    for device in devices:
        pl.semaphore_signal(barrier, inc=1, device_id=device, device_id_type=MESH)
    pl.semaphore_wait(barrier, len(devices))


def gather_kernel(count, chips, *refs):
    shards, wholes = refs[:count], refs[count : 2 * count]
    own_sem, ring_send, ring_recv, pair_send, pair_recv = refs[2 * count :]
    me, core, position, way = ring_place(chips)
    after = {"grp": ring_index(position + way, core, chips)}
    before = {"grp": ring_index(position - way, core, chips)}
    pair = {"grp": me + 1 - 2 * core}
    greet([after, before, pair])

    def ring_copy(step, k, index, source):
        return pltpu.make_async_remote_copy(
            src_ref=source,
            dst_ref=wholes[k].at[index],
            send_sem=ring_send.at[step, k],
            recv_sem=ring_recv.at[step, k],
            device_id=after,
            device_id_type=MESH,
        )

    def pair_copy(step, k, index, source):
        return pltpu.make_async_remote_copy(
            src_ref=source,
            dst_ref=wholes[k].at[index],
            send_sem=pair_send.at[step, k],
            recv_sem=pair_recv.at[step, k],
            device_id=pair,
            device_id_type=MESH,
        )

    for k in range(count):
        ring_copy(0, k, me, shards[k]).start()
        pair_copy(0, k, me, shards[k]).start()
        pltpu.make_async_copy(shards[k], wholes[k].at[me], own_sem.at[k]).start()

    def step_body(step, carry):
        index = ring_index(position - way * step, core, chips)
        for k in range(count):
            ring_copy(step - 1, k, index, wholes[k].at[index]).wait_recv()
            ring_copy(step, k, index, wholes[k].at[index]).start()
            pair_copy(step, k, index, wholes[k].at[index]).start()
        return carry

    lax.fori_loop(1, chips - 1, step_body, 0)
    final = ring_index(position - way * (chips - 1), core, chips)
    for k in range(count):
        ring_copy(chips - 2, k, final, wholes[k].at[final]).wait_recv()
        pair_copy(chips - 1, k, final, wholes[k].at[final]).start()

    def finish(step, carry):
        index = ring_index(position - way * step, core, chips)
        other = ring_index(position + way * step, 1 - core, chips)
        for k in range(count):
            ring_copy(step, k, index, wholes[k].at[index]).wait_send()
            pair_copy(step, k, index, wholes[k].at[index]).wait_send()
            pair_copy(step, k, other, wholes[k].at[other]).wait_recv()
        return carry

    lax.fori_loop(0, chips - 1, finish, 0)
    last_other = ring_index(position + way * (chips - 1), 1 - core, chips)
    for k in range(count):
        pair_copy(chips - 1, k, final, wholes[k].at[final]).wait_send()
        pair_copy(chips - 1, k, last_other, wholes[k].at[last_other]).wait_recv()
        pltpu.make_async_copy(shards[k], wholes[k].at[me], own_sem.at[k]).wait()


def ring_gather(shards, group, collective_id):
    count, chips = len(shards), group // 2
    wholes = pl.pallas_call(
        functools.partial(gather_kernel, count, chips),
        out_shape=[jax.ShapeDtypeStruct((group, *s.shape), s.dtype) for s in shards],
        in_specs=[pl.BlockSpec(memory_space=pl.ANY)] * count,
        out_specs=[pl.BlockSpec(memory_space=pl.ANY)] * count,
        scratch_shapes=[pltpu.SemaphoreType.DMA((count,))]
        + [pltpu.SemaphoreType.DMA((chips, count))] * 4,
        compiler_params=pltpu.CompilerParams(collective_id=collective_id, has_side_effects=True),
    )(*shards)
    return [w.reshape(group * w.shape[1], w.shape[2]) for w in wholes]


def scatter_kernel(count, chips, reps, *refs):
    terms, totals = refs[:count], refs[count : 2 * count]
    held, paired, ringed = (refs[(2 + i) * count : (3 + i) * count] for i in range(3))
    refs = refs[5 * count :]
    own_sem, ring_send, ring_recv, pair_send, pair_recv = refs[:5]
    me, core, position, way = ring_place(chips)
    after = {"grp": ring_index(position + way, core, chips)}
    before = {"grp": ring_index(position - way, core, chips)}
    pair = {"grp": me + 1 - 2 * core}
    rep = lax.axis_index("rep") if reps > 1 else 0
    others = [{"rep": lax.rem(rep + o, reps)} for o in range(1, reps)]
    greet([after, before, pair] + others)

    def own_copy(step, k):
        index = ring_index(position - way * (step + 1), core, chips)
        return pltpu.make_async_copy(
            terms[k].at[index], held[k].at[step], own_sem.at[step, k]
        )

    def pair_copy(step, k):
        index = ring_index(position + way * (step + 1), 1 - core, chips)
        return pltpu.make_async_remote_copy(
            src_ref=terms[k].at[index],
            dst_ref=paired[k].at[step],
            send_sem=pair_send.at[step, k],
            recv_sem=pair_recv.at[step, k],
            device_id=pair,
            device_id_type=MESH,
        )

    def ring_copy(step, k):
        return pltpu.make_async_remote_copy(
            src_ref=held[k].at[step],
            dst_ref=ringed[k].at[step],
            send_sem=ring_send.at[step, k],
            recv_sem=ring_recv.at[step, k],
            device_id=after,
            device_id_type=MESH,
        )

    def start_body(step, carry):
        for k in range(count):
            pair_copy(step, k).start()
            own_copy(step, k).start()
        return carry

    lax.fori_loop(0, chips, start_body, 0)

    def add(k, step, ring_step):
        rows = held[k].shape[1]

        def add_rows(i, carry):
            piece = pl.ds(pl.multiple_of(i * 16, 16), 16)
            value = held[k][step, piece, :].astype(jnp.float32)
            value = value + paired[k][step, piece, :].astype(jnp.float32)
            if ring_step is not None:
                value = value + ringed[k][ring_step, piece, :].astype(jnp.float32)
            held[k][step, piece, :] = value.astype(jnp.bfloat16)
            return carry

        lax.fori_loop(0, rows // 16, add_rows, 0)

    for k in range(count):
        own_copy(0, k).wait()
        pair_copy(0, k).wait_recv()
        add(k, 0, None)
        ring_copy(0, k).start()

    def step_body(step, carry):
        for k in range(count):
            own_copy(step, k).wait()
            pair_copy(step, k).wait_recv()
            ring_copy(step - 1, k).wait_recv()
            add(k, step, step - 1)
            ring_copy(step, k).start()
        return carry

    lax.fori_loop(1, chips - 1, step_body, 0)
    last = chips - 1
    for k in range(count):
        own_copy(last, k).wait()
        pair_copy(last, k).wait_recv()
        ring_copy(last - 1, k).wait_recv()
        add(k, last, last - 1)
        if reps > 1:
            rep_bufs, rep_send, rep_recv = refs[5 : 5 + count], refs[-2], refs[-1]
            for o in range(1, reps):
                pltpu.make_async_remote_copy(
                    src_ref=held[k].at[last],
                    dst_ref=rep_bufs[k].at[rep],
                    send_sem=rep_send.at[o, k],
                    recv_sem=rep_recv.at[o, k],
                    device_id=others[o - 1],
                    device_id_type=MESH,
                ).start()
            rep_bufs[k][rep] = held[k][last]
    for k in range(count):
        if reps > 1:
            for o in range(1, reps):
                pltpu.make_async_remote_copy(
                    src_ref=held[k].at[last],
                    dst_ref=rep_bufs[k].at[lax.rem(rep + reps - o, reps)],
                    send_sem=rep_send.at[o, k],
                    recv_sem=rep_recv.at[o, k],
                    device_id=others[o - 1],
                    device_id_type=MESH,
                ).wait()
            value = rep_bufs[k][0].astype(jnp.float32)
            for o in range(1, reps):
                value = value + rep_bufs[k][o].astype(jnp.float32)
            totals[k][...] = value
        else:
            totals[k][...] = held[k][last].astype(jnp.float32)

    def finish(step, carry):
        for k in range(count):
            pair_copy(step, k).wait_send()
            ring_copy(step, k).wait_send()
        return carry

    lax.fori_loop(0, chips - 1, finish, 0)
    for k in range(count):
        pair_copy(last, k).wait_send()


def ring_scatter(terms, group, reps, collective_id):
    count, chips = len(terms), group // 2
    terms = [t.reshape(group, t.shape[0] // group, t.shape[1]) for t in terms]
    shapes = [t.shape[1:] for t in terms]
    scratch = [pltpu.VMEM((chips, *s), jnp.bfloat16) for s in shapes]
    scratch += [pltpu.VMEM((chips, *s), jnp.bfloat16) for s in shapes]
    scratch += [pltpu.VMEM((chips - 1, *s), jnp.bfloat16) for s in shapes]
    scratch += [pltpu.SemaphoreType.DMA((chips, count))] * 5
    if reps > 1:
        scratch += [pltpu.VMEM((reps, *s), jnp.bfloat16) for s in shapes]
        scratch += [pltpu.SemaphoreType.DMA((reps, count))] * 2
    return pl.pallas_call(
        functools.partial(scatter_kernel, count, chips, reps),
        out_shape=[jax.ShapeDtypeStruct(s, jnp.float32) for s in shapes],
        in_specs=[pl.BlockSpec(memory_space=pl.ANY)] * count,
        out_specs=[pl.BlockSpec(memory_space=pltpu.VMEM)] * count,
        scratch_shapes=scratch,
        compiler_params=pltpu.CompilerParams(
            collective_id=collective_id, has_side_effects=True, vmem_limit_bytes=56 * 2**20
        ),
    )(*terms)


def on_device(
    tokens,
    lengths,
    cotangent,
    attn_gain,
    w_query,
    key_projection,
    value_projection,
    w_out,
    ffn_gain,
    w_gate,
    w_up,
    w_down,
):
    group = lax.axis_size("grp")
    reps = lax.axis_size("rep")
    index = lax.axis_index("grp")
    row_count, width = tokens.shape[1:]
    share = width // group
    padded = -(-share // 16) * 16
    columns = jnp.arange(group * padded, dtype=jnp.int32)
    within = columns % padded
    spread = (
        (columns // padded * share + within)[None, :] == jnp.arange(width, dtype=jnp.int32)[:, None]
    ) & (within < share)[None, :]
    spread = spread.astype(jnp.bfloat16)
    inputs = jnp.dot(tokens[0], spread, preferred_element_type=jnp.float32)
    sequence_length = row_count * group
    block_extent = math.gcd(sequence_length, 512)
    group_ratio = QUERY_HEADS // KEY_VALUE_HEADS
    query_width = QUERY_HEADS * HEAD_WIDTH
    key_width = KEY_VALUE_HEADS * HEAD_WIDTH
    scale = 1.0 / math.sqrt(HEAD_WIDTH)
    lengths_row = lengths[0]
    places = index * row_count + jnp.arange(row_count, dtype=jnp.int32)
    q_docs, q_pos = doc_layout(lengths_row, places)
    angle = q_pos.astype(jnp.float32)[:, None] * frequencies(HEAD_WIDTH)[None, :]
    cosine_table = jnp.cos(angle)[:, None, :]
    sine_table = jnp.sin(angle)[:, None, :]
    count = ((index + 1) * row_count + block_extent - 1) // block_extent
    rows_added = ((0, padded - share), (0, 0))
    first_shard = jnp.concatenate(
        [w_query, key_projection, value_projection, attn_gain[:, None], ffn_gain[:, None]], axis=1
    )
    w_first, w_attn_out, w_g, w_u, w_d = ring_gather(
        [
            jnp.pad(first_shard, rows_added),
            jnp.pad(jnp.transpose(w_out), rows_added),
            jnp.pad(w_gate, rows_added),
            jnp.pad(w_up, rows_added),
            jnp.pad(jnp.transpose(w_down), rows_added),
        ],
        group,
        0,
    )
    qkv_width = query_width + 2 * key_width
    gains = jnp.transpose(w_first[:, qkv_width:]).astype(jnp.float32)
    gain_one, gain_two = gains[0], gains[1]
    w_qkv = w_first[:, :qkv_width]
    inv_one = lax.rsqrt(jnp.sum(inputs * inputs, axis=-1, keepdims=True) / width + EPS)
    first_normalized = (inputs * inv_one * gain_one).astype(jnp.bfloat16)
    projected = jnp.dot(first_normalized, w_qkv, preferred_element_type=jnp.float32)
    q_pre = projected[:, :query_width].reshape(row_count, QUERY_HEADS, HEAD_WIDTH)
    key_unrotated = projected[:, query_width : query_width + key_width].reshape(
        row_count, KEY_VALUE_HEADS, HEAD_WIDTH
    )
    value_rows = projected[:, query_width + key_width :].astype(jnp.bfloat16)
    query_row_block = rotary_apply(q_pre, cosine_table, sine_table).astype(jnp.bfloat16)
    key_row_block = (
        rotary_apply(key_unrotated, cosine_table, sine_table)
        .astype(jnp.bfloat16)
        .reshape(row_count, key_width)
    )
    every_key_row, every_value_row = ring_gather([key_row_block, value_rows], group, 1)
    every_key_row = every_key_row.reshape(sequence_length, KEY_VALUE_HEADS, HEAD_WIDTH)
    every_value_row = every_value_row.reshape(sequence_length, KEY_VALUE_HEADS, HEAD_WIDTH)
    grouped_queries = query_row_block.reshape(row_count, KEY_VALUE_HEADS, group_ratio, HEAD_WIDTH)

    def block_probe(number):
        block_offset = (number * block_extent).astype(jnp.int32)
        key_blk = lax.dynamic_slice_in_dim(every_key_row, block_offset, block_extent, 0)
        value_blk = lax.dynamic_slice_in_dim(every_value_row, block_offset, block_extent, 0)
        k_places = block_offset + jnp.arange(block_extent, dtype=jnp.int32)
        k_docs, _ = doc_layout(lengths_row, k_places)
        allowed = (k_places[None, :] <= places[:, None]) & (k_docs[None, :] == q_docs[:, None])
        logits = (
            jnp.einsum(
                "qgrd,kgd->grqk", grouped_queries, key_blk, preferred_element_type=jnp.float32
            )
            * scale
        )
        return (block_offset, key_blk, value_blk, allowed, logits)

    def out_step(number, carry):
        top, total, summed, extra = carry
        _, _, value_blk, allowed, logits = block_probe(number)
        masked = jnp.where(allowed, logits, NEG)
        new_top = jnp.maximum(top, jnp.max(masked, axis=-1))
        weights = jnp.where(allowed, jnp.exp(masked - new_top[..., None]), 0.0)
        rescale = jnp.exp(top - new_top)
        total = total * rescale + jnp.sum(weights, axis=-1)
        rounded = weights.astype(jnp.bfloat16)
        remainder = (weights - rounded.astype(jnp.float32)).astype(jnp.bfloat16)
        summed = summed * rescale[..., None] + jnp.einsum(
            "grqk,kgd->grqd", rounded, value_blk, preferred_element_type=jnp.float32
        )
        extra = extra * rescale[..., None] + jnp.einsum(
            "grqk,kgd->grqd", remainder, value_blk, preferred_element_type=jnp.float32
        )
        return (new_top, total, summed, extra)

    statistic_shape = (KEY_VALUE_HEADS, group_ratio, row_count)
    out_zero_fill = jnp.zeros((*statistic_shape, HEAD_WIDTH), jnp.float32)
    top, total, attn_out, extra = lax.fori_loop(
        0,
        count,
        out_step,
        (
            jnp.full(statistic_shape, NEG, jnp.float32),
            jnp.zeros(statistic_shape, jnp.float32),
            out_zero_fill,
            out_zero_fill,
        ),
    )
    log_total = top + jnp.log(total)
    head_zero_fill = jnp.zeros((row_count, KEY_VALUE_HEADS, group_ratio, HEAD_WIDTH), jnp.float32)
    attn_out = jnp.transpose(attn_out / total[..., None], (2, 0, 1, 3))
    extra = jnp.transpose(extra / total[..., None], (2, 0, 1, 3))
    exact_out = attn_out + extra
    attn_low = attn_out.reshape(row_count, query_width).astype(jnp.bfloat16)
    mid = inputs + jnp.einsum("tq,dq->td", attn_low, w_attn_out, preferred_element_type=jnp.float32)
    inv_two = lax.rsqrt(jnp.sum(mid * mid, axis=-1, keepdims=True) / width + EPS)
    normed_two = (mid * inv_two * gain_two).astype(jnp.bfloat16)
    gate = jnp.dot(normed_two, w_g, preferred_element_type=jnp.float32)
    up = jnp.dot(normed_two, w_u, preferred_element_type=jnp.float32)
    sig = jax.nn.sigmoid(gate)
    hidden = (gate * sig * up).astype(jnp.bfloat16)
    result = mid + jnp.einsum("tf,df->td", hidden, w_d, preferred_element_type=jnp.float32)
    result = jnp.einsum(
        "td,wd->tw", result.astype(jnp.bfloat16), spread, preferred_element_type=jnp.float32
    )
    grad_out = jnp.dot(cotangent[0], spread, preferred_element_type=jnp.float32)
    grad_low = grad_out.astype(jnp.bfloat16)
    d_wdown_turned = jnp.einsum(
        "td,tf->df", grad_low, hidden, preferred_element_type=jnp.float32
    ).astype(jnp.bfloat16)
    d_hidden = jnp.dot(grad_low, w_d, preferred_element_type=jnp.float32)
    d_gate = (d_hidden * up * sig * (1.0 + gate * (1.0 - sig))).astype(jnp.bfloat16)
    d_up = (d_hidden * gate * sig).astype(jnp.bfloat16)
    d_wgate = jnp.einsum(
        "td,tf->df", normed_two, d_gate, preferred_element_type=jnp.float32
    ).astype(jnp.bfloat16)
    d_wup = jnp.einsum(
        "td,tf->df", normed_two, d_up, preferred_element_type=jnp.float32
    ).astype(jnp.bfloat16)
    d_normed_two = jnp.einsum("tf,df->td", d_gate, w_g, preferred_element_type=jnp.float32)
    d_normed_two = d_normed_two + jnp.einsum(
        "tf,df->td", d_up, w_u, preferred_element_type=jnp.float32
    )
    d_mid, d_gain_two = norm_back(mid, inv_two, gain_two, d_normed_two, width)
    d_mid = d_mid + grad_out
    d_mid_low = d_mid.astype(jnp.bfloat16)
    d_wout_turned = jnp.einsum(
        "td,tq->dq", d_mid_low, attn_low, preferred_element_type=jnp.float32
    ).astype(jnp.bfloat16)
    attention_gradient = jnp.dot(
        d_mid_low, w_attn_out, preferred_element_type=jnp.float32
    ).astype(jnp.bfloat16)
    grouped_gradient = attention_gradient.reshape(
        row_count, KEY_VALUE_HEADS, group_ratio, HEAD_WIDTH
    )
    delta = jnp.transpose(
        jnp.sum(grouped_gradient.astype(jnp.float32) * exact_out, axis=-1), (1, 2, 0)
    )

    def back_step(number, carry):
        d_query, key_gradient, value_gradient = carry
        block_offset, key_blk, value_blk, allowed, logits = block_probe(number)
        probs = jnp.where(allowed, jnp.exp(logits - log_total[..., None]), 0.0)
        d_probs = jnp.einsum(
            "qgrd,kgd->grqk", grouped_gradient, value_blk, preferred_element_type=jnp.float32
        )
        d_scores = (probs * (d_probs - delta[..., None])).astype(jnp.bfloat16)
        d_query = (
            d_query
            + jnp.einsum("grqk,kgd->qgrd", d_scores, key_blk, preferred_element_type=jnp.float32)
            * scale
        )
        key_block_gradient = (
            jnp.einsum(
                "grqk,qgrd->kgd", d_scores, grouped_queries, preferred_element_type=jnp.float32
            )
            * scale
        )
        value_block_gradient = jnp.einsum(
            "grqk,qgrd->kgd",
            probs.astype(jnp.bfloat16),
            grouped_gradient,
            preferred_element_type=jnp.float32,
        )
        key_gradient = lax.dynamic_update_slice_in_dim(
            key_gradient,
            key_block_gradient.reshape(block_extent, KEY_VALUE_HEADS * HEAD_WIDTH),
            block_offset,
            0,
        )
        value_gradient = lax.dynamic_update_slice_in_dim(
            value_gradient,
            value_block_gradient.reshape(block_extent, KEY_VALUE_HEADS * HEAD_WIDTH),
            block_offset,
            0,
        )
        return (d_query, key_gradient, value_gradient)

    key_value_zero_fill = jnp.zeros((sequence_length, KEY_VALUE_HEADS * HEAD_WIDTH), jnp.float32)
    d_query, key_gradient, value_gradient = lax.fori_loop(
        0, count, back_step, (head_zero_fill, key_value_zero_fill, key_value_zero_fill)
    )
    local_key_rows, own_values = ring_scatter(
        [key_gradient.astype(jnp.bfloat16), value_gradient.astype(jnp.bfloat16)], group, 1, 2
    )
    d_q_pre = rotary_apply(
        d_query.reshape(row_count, QUERY_HEADS, HEAD_WIDTH), cosine_table, -sine_table
    ).reshape(row_count, query_width)
    d_k_pre = rotary_apply(
        local_key_rows.reshape(row_count, KEY_VALUE_HEADS, HEAD_WIDTH), cosine_table, -sine_table
    ).reshape(row_count, key_width)
    d_projected = jnp.concatenate([d_q_pre, d_k_pre, own_values], axis=1).astype(jnp.bfloat16)
    d_wqkv = jnp.einsum(
        "td,tq->dq", first_normalized, d_projected, preferred_element_type=jnp.float32
    ).astype(jnp.bfloat16)
    d_normed_one = jnp.einsum("tq,dq->td", d_projected, w_qkv, preferred_element_type=jnp.float32)
    d_inputs, d_gain_one = norm_back(inputs, inv_one, gain_one, d_normed_one, width)
    d_inputs = jnp.einsum(
        "td,wd->tw",
        d_inputs + d_mid,
        spread.astype(jnp.float32),
        precision=lax.Precision.HIGHEST,
        preferred_element_type=jnp.float32,
    )
    d_gains = jnp.stack([d_gain_one, d_gain_two], axis=1).astype(jnp.bfloat16)
    summed = ring_scatter(
        [
            d_wdown_turned,
            d_wgate,
            d_wup,
            d_wout_turned,
            d_wqkv,
            d_gains,
        ],
        group,
        reps,
        3,
    )
    down, d_g, d_u, d_o, first, gain_sums = (s[:share] for s in summed)
    return (
        result[None].astype(jnp.bfloat16),
        d_inputs[None],
        gain_sums[:, 0],
        first[:, :query_width],
        first[:, query_width : query_width + key_width],
        first[:, query_width + key_width :],
        jnp.transpose(d_o),
        gain_sums[:, 1],
        d_g,
        d_u,
        jnp.transpose(down),
    )


def solution(mesh):
    in_specs = (
        P("rep", "grp", None),
        P("rep", None),
        P("rep", "grp", None),
        P("grp"),
        P("grp", None),
        P("grp", None),
        P("grp", None),
        P(None, "grp"),
        P("grp"),
        P("grp", None),
        P("grp", None),
        P(None, "grp"),
    )
    out_specs = (
        P("rep", "grp", None),
        P("rep", "grp", None),
        P("grp"),
        P("grp", None),
        P("grp", None),
        P("grp", None),
        P(None, "grp"),
        P("grp"),
        P("grp", None),
        P("grp", None),
        P(None, "grp"),
    )
    return jax.shard_map(
        on_device, mesh=mesh, in_specs=in_specs, out_specs=out_specs, check_vma=False
    )
```

profile of v0, /device:TPU:1, one launch (start us, length us, event | category | flops | bytes accessed | tf_op | source)
XLA Modules:
  0.0 459.9 jit_solution(2073790606664483037)
XLA Ops:
  1.6 1.3 multiply_reduce_fusion.5
  4.5 1.1 concatenate.30
  9.1 108.9 %shard_map.203 = (bf16[16,64,1602]{2,1,0:T(8,128)(2,1)}, bf16[16,64,960]{2,1,0:T(8,128)(2,1)}, bf16[16,64,2560]{2,1,0:T(8,128)(2,1)}, bf16[16,64,2560]{2,1,0:T(8,128)(2,1)}, bf16[16,64,2560]{2,1,0:T(8,128)(2,1)}) custom-call(bf16[64,1602]{1,0:T(8,128)(2,1)} %pad.18.refs_0_, bf16[64,960]{1,0:T(8,128)(2,1)} %pad.19.refs_1_, bf16[64,2560]{1,0:T(8,128)(2,1)} %pad.20.refs_2_, ...), custom_call_target="tpu_custom_call" | custom-call | tf_op jit(solution)/shard_map/pallas_call | solution.py:146
  118.5 1.1 slice_convert_fusion
  119.9 3.5 fusion.65
  125.2 31.4 %shard_map.204 = (bf16[16,128,320]{2,1,0:T(8,128)(2,1)}, bf16[16,128,320]{2,1,0:T(8,128)(2,1)}) custom-call(bf16[128,320]{1,0:T(8,128)(2,1)} %copy.135.refs_0_, bf16[128,320]{1,0:T(8,128)(2,1)} %copy.168.refs_1_), custom_call_target="tpu_custom_call" | custom-call | tf_op jit(solution)/shard_map/pallas_call | solution.py:146
  156.7 2.3 copy.136
  159.7 2.2 copy.137
  161.9 1.4 reshape_reshape.7
  163.4 4.9 %while.38 = (s32[]{:T(128)}, f32[5,3,128]{2,1,0:T(4,128)S(1)}, f32[5,3,128]{2,1,0:T(4,128)S(1)}, f32[5,3,128,64]{2,3,1,0:T(8,128)S(1)}, f32[5,3,128,64]{2,3,1,0:...) while((s32[]{:T(128)}, f32[5,3,128]{2,1,0:T(4,128)S(1)}, ...), condition=%wide.region_9.10_spmd.clone, body=%wide.region_5.9_spmd.clone.sunk | while | flops 398829440 | bytes 24654604 | solution.py:419
  164.6 0.9 fusion.185
  165.6 1.2 fusion.186
  166.7 1.3 fusion.187
  169.2 2.4 multiply_reduce_fusion.4
  171.8 3.5 fusion.127
  175.3 3.5 fusion.128
  178.8 1.3 fusion.78
  180.1 2.7 multiply_convert_fusion
  182.9 6.4 %fusion.88 = bf16[1,128,960]{1,2,0:T(8,128)(2,1)} fusion(s32[1024]{0:T(1024)S(1)} %fusion.118, pred[1024]{0:T(1024)(128)(4,1)S(1)} %fusion.119, f32[128,1024]{0,1:T(8,128)S(1)} %get-tuple-element.598, bf16[128,2560]{1,0:T(8,128)(2,1)} %get-tuple-element.575, bf16[1024,2560]{1,0:T(8,128)(2,1)} %bitcast.284), kind=kOutput, calls=%fused_computation.102 | convolution fusion | flops 925097984 | bytes 6673408 | tf_op jit(solution)/shard_map/td,wd->tw/dot_general | solution.py:444
  189.2 4.3 fusion.129
  193.5 4.2 multiply_reduce_fusion
  197.9 2.5 convolution_convert_fusion.5
  200.5 1.2 fusion.97
  201.8 1.2 broadcast_in_dim.138
  203.0 1.2 broadcast_in_dim.138.clone
  204.3 6.5 %while.39 = (s32[]{:T(128)}, f32[128,5,3,64]{0,3,2,1:T(8,128)S(1)}, bf16[2048,320]{0,1:T(8,128)(2,1)}, bf16[2048,320]{0,1:T(8,128)(2,1)}, s32[]{:T(128)}, /*inde...) while((s32[]{:T(128)}, f32[128,5,3,64]{0,3,2,1:T(8,128)S(1)}, ...), condition=%wide.region_15.16_spmd.clone, body=%wide.region_13.15_spmd.clone.sunk | while | flops 639752320 | bytes 23824672 | solution.py:521
  205.3 2.3 fusion.199
  209.8 0.9 constant_dynamic-update-slice_fusion.3
  210.7 11.8 %copy.142 = bf16[2048,320]{1,0:T(8,128)(2,1)} copy(bf16[2048,320]{0,1:T(8,128)(2,1)} %get-tuple-element.411) | data formatting | bytes 2621440 | tf_op jit(solution)/shard_map/convert_element_type | solution.py:525
  222.6 2.6 copy.143
  225.2 58.7 %shard_map.205 = (f32[128,320]{1,0:T(8,128)}, f32[128,320]{1,0:T(8,128)}) custom-call(bf16[16,128,320]{2,1,0:T(8,128)(2,1)} %bitcast.245, bf16[16,128,320]{2,1,0:T(8,128)(2,1)} %bitcast.246), custom_call_target="tpu_custom_call" | custom-call | tf_op jit(solution)/shard_map/pallas_call | solution.py:294
  283.9 0.9 convert.54
  285.0 1.1 copy.144
  286.3 3.2 multiply_reduce_fusion.1
  289.5 2.9 fusion.81
  292.5 3.8 convolution_convert_fusion.2
  296.3 3.9 convolution_convert_fusion.1
  300.2 3.9 convolution_convert_fusion
  304.7 2.5 copy.147
  307.3 2.3 convolution_convert_fusion.3
  309.5 3.6 copy.148
  314.2 134.1 %shard_map.206 = (f32[64,2560]{1,0:T(8,128)}, f32[64,2560]{1,0:T(8,128)}, f32[64,2560]{1,0:T(8,128)}, f32[64,960]{1,0:T(8,128)}, f32[64,1600]{1,0:T(8,128)}, /*index=5*/f32[64,2]{1,0:T(8,128)}) custom-call(bf16[16,64,2560]{2,1,0:T(8,128)(2,1)} %bitcast.232, bf16[16,64,2560]{2,1,0:T(8,128)(2,1)} %bitcast.233, bf16[16,64,2560]{2,1,0:T(8,128)(2,1)} %bitcast.234, ...), custom_call_target="tpu_custom_call" | custom-call | tf_op jit(solution)/shard_map/pallas_call | solution.py:294
  448.4 1.5 slice_reduce_fusion
  449.9 1.7 slice.96
  451.6 1.7 fusion.125
  453.3 1.7 slice_bitcast_fusion.1
  455.0 2.0 slice_bitcast_fusion
  456.9 2.0 copy.201
  (132 shorter events, 17.7 us)
Async XLA Ops:
  0.6 1.0 copy-start
  0.7 5.6 %copy-start.26 = (bf16[960,60]{0,1:T(8,128)(2,1)S(1)}, bf16[960,60]{0,1:T(8,128)(2,1)}, u32[]{:S(2)}) copy-start(bf16[960,60]{0,1:T(8,128)(2,1)} %param.23) | copy-start | bytes 345604
  0.7 6.2 %copy-start.21 = (bf16[60,2560]{1,0:T(8,128)(2,1)S(1)}, bf16[60,2560]{1,0:T(8,128)(2,1)}, u32[]{:S(2)}) copy-start(bf16[60,2560]{1,0:T(8,128)(2,1)} %param.25) | copy-start | bytes 921604
  0.7 7.0 %copy-start.22 = (bf16[60,2560]{1,0:T(8,128)(2,1)S(1)}, bf16[60,2560]{1,0:T(8,128)(2,1)}, u32[]{:S(2)}) copy-start(bf16[60,2560]{1,0:T(8,128)(2,1)} %param.26) | copy-start | bytes 921604
  0.7 7.7 %copy-start.23 = (bf16[2560,60]{0,1:T(8,128)(2,1)S(1)}, bf16[2560,60]{0,1:T(8,128)(2,1)}, u32[]{:S(2)}) copy-start(bf16[2560,60]{0,1:T(8,128)(2,1)} %param.27) | copy-start | bytes 921604
  0.7 117.4 %copy-start.27 = (s32[1,4]{1,0:T(1,128)S(1)}, s32[1,4]{1,0:T(1,128)}, u32[]{:S(2)}) copy-start(s32[1,4]{1,0:T(1,128)} %param.17) | copy-start | bytes 52
  2.9 120.5 %copy-start.2 = (f32[128,1024]{0,1:T(8,128)}, f32[128,1024]{0,1:T(8,128)S(1)}, u32[]{:S(2)}) copy-start(f32[128,1024]{0,1:T(8,128)S(1)} %get-tuple-element.596) | copy-start | bytes 1572868
  123.4 33.2 %copy-start.14 = (f32[128,1600]{0,1:T(8,128)}, f32[128,1600]{0,1:T(8,128)S(1)}, u32[]{:S(2)}) copy-start(f32[128,1600]{0,1:T(8,128)S(1)} %fusion.65) | copy-start | bytes 2457604
  156.6 2.9 slice-start
  163.4 5.7 %copy-start.3 = (f32[128,1024]{0,1:T(8,128)S(1)}, f32[128,1024]{0,1:T(8,128)}, u32[]{:S(2)}) copy-start(f32[128,1024]{0,1:T(8,128)} %copy-done.2) | copy-start | bytes 1572868
  163.8 1.8 copy-start.15
  168.3 0.8 copy-start.13
  169.1 2.4 copy-start.11
  171.8 8.3 %slice-start.1 = ((s8[5242880]{0:T(1024)(128)(4,1)}), s8[4194304]{0:T(1024)(128)(4,1)S(1)}, s32[]{:S(2)}) async-start(s8[5242880]{0:T(1024)(128)(4,1)} %bitcast.285), calls=%async_computation.1 | async-start | bytes 8388608
  175.3 3.5 copy-start.28
  175.3 4.8 %slice-start.2 = ((s8[5242880]{0:T(1024)(128)(4,1)}), s8[1048576]{0:T(1024)(128)(4,1)S(1)}, s32[]{:S(2)}) async-start(s8[5242880]{0:T(1024)(128)(4,1)} %bitcast.285), calls=%async_computation.2 | async-start | bytes 2097152
  180.1 2.7 copy-start.5
  189.2 4.3 copy-start.9
  193.5 4.2 copy-start.6
  200.5 1.3 copy-start.16
  204.3 1.1 copy-start.17
  222.6 63.7 %copy-start.4 = (f32[128,1024]{0,1:T(8,128)S(1)}, f32[128,1024]{0,1:T(8,128)}, u32[]{:S(2)}) copy-start(f32[128,1024]{0,1:T(8,128)} %copy-done.2) | copy-start | bytes 1572868
  285.0 4.5 copy-start.24
  286.1 3.4 copy-start.25
  286.2 3.3 copy-start.18
  286.3 6.2 %copy-start.19 = (bf16[128,2560]{1,0:T(8,128)(2,1)S(1)}, bf16[128,2560]{1,0:T(8,128)(2,1)}, u32[]{:S(2)}) copy-start(bf16[128,2560]{1,0:T(8,128)(2,1)} %get-tuple-element.575) | copy-start | bytes 1966084
  289.5 3.0 copy-start.7
  292.5 3.8 copy-start.8
  296.3 3.9 copy-start.10
  300.2 3.9 copy-start.12
  314.2 145.5 %copy-start.1 = (bf16[1,128,960]{1,2,0:T(8,128)(2,1)S(1)}, bf16[1,128,960]{1,2,0:T(8,128)(2,1)}, u32[]{:S(2)}) copy-start(bf16[1,128,960]{1,2,0:T(8,128)(2,1)} %param.16) | copy-start | bytes 737284
  448.4 10.6 %copy-start.20 = (f32[64,2560]{1,0:T(8,128)S(1)}, f32[64,2560]{1,0:T(8,128)}, u32[]{:S(2)}) copy-start(f32[64,2560]{1,0:T(8,128)} %get-tuple-element.419) | copy-start | bytes 1966084
where the time goes:
time: 469 us; the launch traced here: 460 us
  Pallas kernels  333 us (71%)
  matrix products  64.6 us (14%)
  local copies, waits for them, and re-layouts  54 us (12%)
  other arithmetic  6.22 us (1%)
    pallas_call x2, Pallas kernels, ring_scatter(): pl.pallas_call(functools.partial(scatter_kernel, count, chips, reps), out...  193 us
    pallas_call x2, Pallas kernels, ring_gather(): pl.pallas_call(functools.partial(gather_kernel, count, chips), out_shape=...  140 us
    convert_element_type x1, local copies, waits for them, and re-layouts, on_device(): key_gradient.astype(jnp.bfloat16)  11.8 us

commit v1 on v0

--- a/solution.py
+++ b/solution.py
@@ -76,83 +76,150 @@
     pl.semaphore_wait(barrier, len(devices))
 
 
-def gather_kernel(count, chips, *refs):
+def gather_kernel(count, chips, crossing, *refs):
     shards, wholes = refs[:count], refs[count : 2 * count]
-    own_sem, ring_send, ring_recv, pair_send, pair_recv = refs[2 * count :]
+    own_sem, ring_send, ring_recv, pair_send, pair_recv = refs[2 * count : 2 * count + 5]
     me, core, position, way = ring_place(chips)
     after = {"grp": ring_index(position + way, core, chips)}
     before = {"grp": ring_index(position - way, core, chips)}
     pair = {"grp": me + 1 - 2 * core}
-    greet([after, before, pair])
-
-    def ring_copy(step, k, index, source):
+    partners = [after, before, pair]
+    if crossing:
+        cross_send, cross_recv, swap_send, swap_recv = refs[2 * count + 5 :]
+        rep = lax.axis_index("rep")
+        plane = lax.rem(rep, 2)
+        across = {"rep": rep + 1 - 2 * plane}
+        partners.append(across)
+    greet(partners)
+    wide = count - 1 if crossing else count
+
+    def shard(k):
+        return shards[k].at[plane] if k == wide else shards[k]
+
+    def whole(k, index):
+        return wholes[k].at[plane, index] if k == wide else wholes[k].at[index]
+
+    def copy(source, target, sends, receives, device):
         return pltpu.make_async_remote_copy(
             src_ref=source,
-            dst_ref=wholes[k].at[index],
-            send_sem=ring_send.at[step, k],
-            recv_sem=ring_recv.at[step, k],
-            device_id=after,
+            dst_ref=target,
+            send_sem=sends,
+            recv_sem=receives,
+            device_id=device,
             device_id_type=MESH,
         )
 
-    def pair_copy(step, k, index, source):
-        return pltpu.make_async_remote_copy(
-            src_ref=source,
-            dst_ref=wholes[k].at[index],
-            send_sem=pair_send.at[step, k],
-            recv_sem=pair_recv.at[step, k],
-            device_id=pair,
-            device_id_type=MESH,
-        )
-
+    def ring_copy(step, k, index, source=None):
+        source = whole(k, index) if source is None else source
+        sems = (ring_send.at[step, k], ring_recv.at[step, k])
+        return copy(source, whole(k, index), *sems, after)
+
+    def pair_copy(step, k, index, source=None):
+        source = whole(k, index) if source is None else source
+        sems = (pair_send.at[step, k], pair_recv.at[step, k])
+        return copy(source, whole(k, index), *sems, pair)
+
+    def cross_copy(step, index):
+        sems = (cross_send.at[step], cross_recv.at[step])
+        return copy(whole(wide, index), whole(wide, index), *sems, across)
+
+    def cross_landed(step, index):
+        target = wholes[wide].at[1 - plane, index]
+        copy(target, target, cross_send.at[step], cross_recv.at[step], across).wait_recv()
+
+    def swap_copy(step, index, source=None):
+        target = wholes[wide].at[1 - plane, index]
+        source = target if source is None else source
+        return copy(source, target, swap_send.at[step], swap_recv.at[step], pair)
+
+    own_copies = [
+        pltpu.make_async_copy(shard(k), whole(k, me), own_sem.at[k]) for k in range(count)
+    ]
+    if crossing:
+        other_plane = shards[wide].at[1 - plane]
+        own_copies.append(
+            pltpu.make_async_copy(
+                other_plane, wholes[wide].at[1 - plane, me], own_sem.at[count]
+            )
+        )
     for k in range(count):
-        ring_copy(0, k, me, shards[k]).start()
-        pair_copy(0, k, me, shards[k]).start()
-        pltpu.make_async_copy(shards[k], wholes[k].at[me], own_sem.at[k]).start()
-
-    def step_body(step, carry):
+        ring_copy(0, k, me, shard(k)).start()
+        pair_copy(0, k, me, shard(k)).start()
+    if crossing:
+        swap_copy(0, me, other_plane).start()
+    for own_copy in own_copies:
+        own_copy.start()
+
+    def swap_step(step):
+        index = ring_index(position - way * step, core, chips)
+        cross_landed(step, index)
+        swap_copy(step, index).start()
+
+    def step_body(step, carry, lag):
         index = ring_index(position - way * step, core, chips)
         for k in range(count):
-            ring_copy(step - 1, k, index, wholes[k].at[index]).wait_recv()
-            ring_copy(step, k, index, wholes[k].at[index]).start()
-            pair_copy(step, k, index, wholes[k].at[index]).start()
+            ring_copy(step - 1, k, index).wait_recv()
+            ring_copy(step, k, index).start()
+            pair_copy(step, k, index).start()
+        if crossing:
+            cross_copy(step, index).start()
+            if lag:
+                swap_step(step - lag)
         return carry
 
-    lax.fori_loop(1, chips - 1, step_body, 0)
+    lax.fori_loop(1, 3, functools.partial(step_body, lag=0), 0)
+    lax.fori_loop(3, chips - 1, functools.partial(step_body, lag=2), 0)
     final = ring_index(position - way * (chips - 1), core, chips)
     for k in range(count):
-        ring_copy(chips - 2, k, final, wholes[k].at[final]).wait_recv()
-        pair_copy(chips - 1, k, final, wholes[k].at[final]).start()
+        ring_copy(chips - 2, k, final).wait_recv()
+        pair_copy(chips - 1, k, final).start()
+    if crossing:
+        cross_copy(chips - 1, final).start()
+        for step in range(chips - 3, chips):
+            swap_step(step)
 
     def finish(step, carry):
         index = ring_index(position - way * step, core, chips)
         other = ring_index(position + way * step, 1 - core, chips)
         for k in range(count):
-            ring_copy(step, k, index, wholes[k].at[index]).wait_send()
-            pair_copy(step, k, index, wholes[k].at[index]).wait_send()
-            pair_copy(step, k, other, wholes[k].at[other]).wait_recv()
+            ring_copy(step, k, index).wait_send()
+            pair_copy(step, k, index).wait_send()
+            pair_copy(step, k, other).wait_recv()
+        if crossing:
+            swap_copy(step, index).wait_send()
+            swap_copy(step, other).wait_recv()
+            cross_copy(step + 1, index).wait_send()
         return carry
 
     lax.fori_loop(0, chips - 1, finish, 0)
     last_other = ring_index(position + way * (chips - 1), 1 - core, chips)
     for k in range(count):
-        pair_copy(chips - 1, k, final, wholes[k].at[final]).wait_send()
-        pair_copy(chips - 1, k, last_other, wholes[k].at[last_other]).wait_recv()
-        pltpu.make_async_copy(shards[k], wholes[k].at[me], own_sem.at[k]).wait()
-
-
-def ring_gather(shards, group, collective_id):
+        pair_copy(chips - 1, k, final).wait_send()
+        pair_copy(chips - 1, k, last_other).wait_recv()
+    if crossing:
+        swap_copy(chips - 1, final).wait_send()
+        swap_copy(chips - 1, last_other).wait_recv()
+    for own_copy in own_copies:
+        own_copy.wait()
+
+
+def ring_gather(shards, group, collective_id, crossing=False):
     count, chips = len(shards), group // 2
+    shapes = [(group, *s.shape) for s in shards]
+    scratch = [pltpu.SemaphoreType.DMA((count + 1,))]
+    scratch += [pltpu.SemaphoreType.DMA((chips, count))] * 4
+    if crossing:
+        shapes[-1] = (2, group, *shards[-1].shape[1:])
+        scratch += [pltpu.SemaphoreType.DMA((chips,))] * 4
     wholes = pl.pallas_call(
-        functools.partial(gather_kernel, count, chips),
-        out_shape=[jax.ShapeDtypeStruct((group, *s.shape), s.dtype) for s in shards],
+        functools.partial(gather_kernel, count, chips, crossing),
+        out_shape=[jax.ShapeDtypeStruct(s, jnp.bfloat16) for s in shapes],
         in_specs=[pl.BlockSpec(memory_space=pl.ANY)] * count,
         out_specs=[pl.BlockSpec(memory_space=pl.ANY)] * count,
-        scratch_shapes=[pltpu.SemaphoreType.DMA((count,))]
-        + [pltpu.SemaphoreType.DMA((chips, count))] * 4,
+        scratch_shapes=scratch,
         compiler_params=pltpu.CompilerParams(collective_id=collective_id, has_side_effects=True),
     )(*shards)
-    return [w.reshape(group * w.shape[1], w.shape[2]) for w in wholes]
+    return [w.reshape(*w.shape[:-3], group * w.shape[-2], w.shape[-1]) for w in wholes]
 
 
 def scatter_kernel(count, chips, reps, *refs):
@@ -347,17 +414,21 @@
     first_shard = jnp.concatenate(
         [w_query, key_projection, value_projection, attn_gain[:, None], ffn_gain[:, None]], axis=1
     )
-    w_first, w_attn_out, w_g, w_u, w_d = ring_gather(
-        [
-            jnp.pad(first_shard, rows_added),
-            jnp.pad(jnp.transpose(w_out), rows_added),
-            jnp.pad(w_gate, rows_added),
-            jnp.pad(w_up, rows_added),
-            jnp.pad(jnp.transpose(w_down), rows_added),
-        ],
-        group,
-        0,
-    )
+    narrow_shards = [
+        jnp.pad(first_shard, rows_added),
+        jnp.pad(jnp.transpose(w_out), rows_added),
+        jnp.pad(jnp.transpose(w_down), rows_added),
+    ]
+    gate_shard, up_shard = jnp.pad(w_gate, rows_added), jnp.pad(w_up, rows_added)
+    if reps % 2 == 0:
+        w_first, w_attn_out, w_d, w_both = ring_gather(
+            [*narrow_shards, jnp.stack([gate_shard, up_shard])], group, 0, True
+        )
+        w_g, w_u = w_both[0], w_both[1]
+    else:
+        w_first, w_attn_out, w_d, w_g, w_u = ring_gather(
+            [*narrow_shards, gate_shard, up_shard], group, 0
+        )
     qkv_width = query_width + 2 * key_width
     gains = jnp.transpose(w_first[:, qkv_width:]).astype(jnp.float32)
     gain_one, gain_two = gains[0], gains[1]

time: 469 us -> 443 us (0.945)
  Pallas kernels: 333 us -> 317 us
  matrix products: 64.6 us -> 56.4 us
    pallas_call x2, Pallas kernels: 140 us -> 126 us  [ring_gather(): pl.pallas_call(functools.partial(gather_kernel, count, chips, crossing),...]
    convert_element_type x1, local copies, waits for them, and re-layouts: 11.8 us -> 1.59 us  [on_device(): key_gradient.astype(jnp.bfloat16)]
    slice x0 -> x1, local copies, waits for them, and re-layouts: none -> 9.18 us  [on_device(): w_g, w_u = (w_both[0], w_both[1])]
where the time goes in v1:
time: 443 us; the launch traced here: 434 us
  Pallas kernels  317 us (72%)
  matrix products  56.4 us (13%)
  local copies, waits for them, and re-layouts  51.8 us (12%)
  other arithmetic  6.05 us (1%)
    pallas_call x2, Pallas kernels, ring_scatter(): pl.pallas_call(functools.partial(scatter_kernel, count, chips, reps), out...  192 us
    pallas_call x2, Pallas kernels, ring_gather(): pl.pallas_call(functools.partial(gather_kernel, count, chips, crossing),...  126 us
    slice x1, local copies, waits for them, and re-layouts, on_device(): w_g, w_u = (w_both[0], w_both[1])  9.18 us

profile of v1, /device:TPU:1, one launch (start us, length us, event | category | flops | bytes accessed | tf_op | source)
XLA Modules:
  0.0 434.0 jit_solution(11335130618909937578)
XLA Ops:
  0.7 1.2 pad_bitcast_fusion
  4.3 1.1 concatenate.30
  6.1 1.7 pad.20.refs_2_
  8.4 93.1 %shard_map.203 = (bf16[16,64,1602]{2,1,0:T(8,128)(2,1)}, bf16[16,64,960]{2,1,0:T(8,128)(2,1)}, bf16[16,64,2560]{2,1,0:T(8,128)(2,1)}, bf16[2,16,64,2560]{3,2,1,0:T(8,128)(2,1)}) custom-call(bf16[64,1602]{1,0:T(8,128)(2,1)} %pad.18.refs_0_, bf16[64,960]{1,0:T(8,128)(2,1)} %pad.19.refs_1_, bf16[64,2560]{1,0:T(8,128)(2,1)} %pad.20.refs_2_, ...), custom_call_target="tpu_custom_call" | custom-call | tf_op jit(solution)/shard_map/pallas_call | solution.py:214
  101.5 1.1 slice_convert_fusion
  102.9 1.3 multiply_reduce_fusion.5
  104.2 3.7 fusion.65
  110.0 32.5 %shard_map.204 = (bf16[16,128,320]{2,1,0:T(8,128)(2,1)}, bf16[16,128,320]{2,1,0:T(8,128)(2,1)}) custom-call(bf16[128,320]{1,0:T(8,128)(2,1)} %copy.135.refs_0_, bf16[128,320]{1,0:T(8,128)(2,1)} %copy.168.refs_1_), custom_call_target="tpu_custom_call" | custom-call | tf_op jit(solution)/shard_map/pallas_call | solution.py:214
  142.5 2.2 copy.136
  145.3 2.2 copy.137
  147.5 1.4 reshape_reshape.7
  149.0 1.1 slice.121
  150.4 4.8 %while.38 = (s32[]{:T(128)}, f32[5,3,128]{2,1,0:T(4,128)S(1)}, f32[5,3,128]{2,1,0:T(4,128)S(1)}, f32[5,3,128,64]{2,3,1,0:T(8,128)S(1)}, f32[5,3,128,64]{2,3,1,0:...) while((s32[]{:T(128)}, f32[5,3,128]{2,1,0:T(4,128)S(1)}, ...), condition=%wide.region_9.10_spmd.clone, body=%wide.region_5.9_spmd.clone.sunk | while | flops 398829440 | bytes 24654596 | solution.py:490
  151.6 0.9 fusion.186
  152.6 1.3 fusion.188
  153.9 1.2 fusion.187
  156.1 2.4 multiply_reduce_fusion.4
  158.7 9.2 %fusion.125 = (bf16[1,16,64,2560]{3,2,1,0:T(8,128)(2,1)}, bf16[1,16,64,2560]{3,2,1,0:T(8,128)(2,1)}) fusion(bf16[2,16,64,2560]{3,2,1,0:T(8,128)(2,1)} %get-tuple-element.404), kind=kLoop, calls=%fused_computation.189 | loop fusion | bytes 20971520 | tf_op jit(solution)/shard_map/slice | solution.py:427
  167.9 3.5 fusion.129
  173.1 1.3 fusion.78
  174.5 2.3 multiply_convert_fusion
  176.8 1.5 fusion.130
  178.3 1.7 multiply_reduce_fusion
  180.3 0.9 convolution_convert_fusion.5
  182.1 1.2 broadcast_in_dim.138.clone
  183.4 6.6 %while.39 = (s32[]{:T(128)}, f32[128,5,3,64]{0,3,2,1:T(8,128)S(1)}, bf16[2048,320]{0,1:T(8,128)(2,1)S(1)}, bf16[2048,320]{0,1:T(8,128)(2,1)}, s32[]{:T(128)}, /*...) while((s32[]{:T(128)}, f32[128,5,3,64]{0,3,2,1:T(8,128)S(1)}, ...), condition=%wide.region_15.16_spmd.clone, body=%wide.region_13.15_spmd.clone.sunk | while | flops 639752320 | bytes 23824664 | solution.py:592
  184.4 2.3 fusion.200
  190.1 1.6 copy.142
  191.7 1.6 copy.143
  193.2 57.1 %shard_map.205 = (f32[128,320]{1,0:T(8,128)}, f32[128,320]{1,0:T(8,128)}) custom-call(bf16[16,128,320]{2,1,0:T(8,128)(2,1)} %bitcast.251, bf16[16,128,320]{2,1,0:T(8,128)(2,1)} %bitcast.252), custom_call_target="tpu_custom_call" | custom-call | tf_op jit(solution)/shard_map/pallas_call | solution.py:361
  250.4 1.0 copy.144
  251.5 1.0 convert.54
  252.6 3.9 multiply_reduce_fusion.1
  257.5 2.2 convolution_convert_fusion.3
  259.7 3.7 copy.148
  263.4 1.8 convolution_convert_fusion.4
  265.2 2.6 copy.147
  267.9 3.9 convolution_convert_fusion
  271.7 3.8 convolution_convert_fusion.1
  275.6 3.8 convolution_convert_fusion.2
  279.3 134.7 %shard_map.206 = (f32[64,2560]{1,0:T(8,128)}, f32[64,2560]{1,0:T(8,128)}, f32[64,2560]{1,0:T(8,128)}, f32[64,960]{1,0:T(8,128)}, f32[64,1600]{1,0:T(8,128)}, /*index=5*/f32[64,2]{1,0:T(8,128)}) custom-call(bf16[16,64,2560]{2,1,0:T(8,128)(2,1)} %bitcast.244, bf16[16,64,2560]{2,1,0:T(8,128)(2,1)} %bitcast.243, bf16[16,64,2560]{2,1,0:T(8,128)(2,1)} %bitcast.242, ...), custom_call_target="tpu_custom_call" | custom-call | tf_op jit(solution)/shard_map/pallas_call | solution.py:361
  414.1 2.0 slice_bitcast_fusion
  416.1 1.7 slice.106
  417.8 1.7 slice_bitcast_fusion.1
  419.4 1.7 fusion.126
  421.2 1.5 slice_reduce_fusion
  422.7 2.9 fusion.81
  425.7 6.2 %fusion.88 = bf16[1,128,960]{1,2,0:T(8,128)(2,1)} fusion(s32[1024]{0:T(1024)S(1)} %fusion.118, pred[1024]{0:T(1024)(128)(4,1)S(1)} %fusion.119, f32[128,1024]{0,1:T(8,128)S(1)} %copy-done.7, bf16[128,2560]{1,0:T(8,128)(2,1)S(1)} %copy-done.28, bf16[1024,2560]{1,0:T(8,128)(2,1)} %bitcast.290), kind=kOutput, calls=%fused_computation.102 | convolution fusion | flops 925097984 | bytes 6673408 | tf_op jit(solution)/shard_map/td,wd->tw/dot_general | solution.py:515
  (153 shorter events, 19.0 us)
Async XLA Ops:
  0.6 102.2 %copy-start = (bf16[1,128,960]{1,2,0:T(8,128)(2,1)S(1)}, bf16[1,128,960]{1,2,0:T(8,128)(2,1)}, u32[]{:S(2)}) copy-start(bf16[1,128,960]{1,2,0:T(8,128)(2,1)} %param.16) | copy-start | bytes 737284
  0.7 7.1 %copy-start.33 = (bf16[960,60]{0,1:T(8,128)(2,1)S(1)}, bf16[960,60]{0,1:T(8,128)(2,1)}, u32[]{:S(2)}) copy-start(bf16[960,60]{0,1:T(8,128)(2,1)} %param.23) | copy-start | bytes 345604
  102.9 5.1 %copy-start.34 = (s32[1,4]{1,0:T(1,128)S(1)}, s32[1,4]{1,0:T(1,128)}, u32[]{:S(2)}) copy-start(s32[1,4]{1,0:T(1,128)} %param.17) | copy-start | bytes 52
  104.2 51.9 %copy-start.11 = (f32[128,1024]{0,1:T(8,128)}, f32[128,1024]{0,1:T(8,128)S(1)}, u32[]{:S(2)}) copy-start(f32[128,1024]{0,1:T(8,128)S(1)} %get-tuple-element.596) | copy-start | bytes 1572868
  107.9 34.5 %copy-start.27 = (f32[128,1600]{0,1:T(8,128)}, f32[128,1600]{0,1:T(8,128)S(1)}, u32[]{:S(2)}) copy-start(f32[128,1600]{0,1:T(8,128)S(1)} %fusion.65) | copy-start | bytes 2457604
  150.8 1.8 copy-start.24
  155.2 0.8 copy-start.22
  156.1 2.4 copy-start.20
  158.5 21.5 %copy-start.6 = (f32[128,1024]{0,1:T(8,128)}, f32[128,1024]{0,1:T(8,128)S(1)}, u32[]{:S(2)}) copy-start(f32[128,1024]{0,1:T(8,128)S(1)} %get-tuple-element.598) | copy-start | bytes 1572868
  158.7 12.7 %copy-start.3 = (bf16[128,1024]{0,1:T(8,128)(2,1)}, bf16[128,1024]{0,1:T(8,128)(2,1)S(1)}, u32[]{:S(2)}) copy-start(bf16[128,1024]{0,1:T(8,128)(2,1)S(1)} %multiply_convert_fusion.3) | copy-start | bytes 786436
  167.9 4.0 copy-start.2
  167.9 6.5 %slice-start.2 = ((s8[5242880]{0:T(1024)(128)(4,1)}), s8[4194304]{0:T(1024)(128)(4,1)S(1)}, s32[]{:S(2)}) async-start(s8[5242880]{0:T(1024)(128)(4,1)} %bitcast.291), calls=%async_computation.2 | async-start | bytes 8388608
  171.4 1.7 copy-start.35
  172.0 2.5 slice-start.3
  173.1 5.2 %slice-start = ((s8[5242880]{0:T(1024)(128)(4,1)}), s8[4194304]{0:T(1024)(128)(4,1)S(1)}, s32[]{:S(2)}) async-start(s8[5242880]{0:T(1024)(128)(4,1)} %bitcast.238), calls=%async_computation | async-start | bytes 8388608
  174.4 5.6 %copy-start.14 = (f32[128,1024]{0,1:T(8,128)}, f32[128,1024]{0,1:T(8,128)S(1)}, u32[]{:S(2)}) copy-start(f32[128,1024]{0,1:T(8,128)S(1)} %fusion.78) | copy-start | bytes 1572868
  174.5 3.8 slice-start.1
  176.8 3.2 copy-start.16
  176.8 3.2 copy-start.18
  178.3 2.0 copy-start.5
  180.0 1.3 copy-start.23
  180.3 1.0 copy-start.9
  181.3 0.7 copy-start.25
  183.4 1.1 copy-start.26
  190.0 1.7 copy-start.8
  191.7 60.9 %copy-start.12 = (f32[128,1024]{0,1:T(8,128)S(1)}, f32[128,1024]{0,1:T(8,128)}, u32[]{:S(2)}) copy-start(f32[128,1024]{0,1:T(8,128)} %copy-done.11) | copy-start | bytes 1572868
  251.5 5.0 %copy-start.31 = (bf16[128,5,64]{0,2,1:T(8,128)(2,1)}, bf16[128,5,64]{0,2,1:T(8,128)(2,1)S(1)}, u32[]{:S(2)}) copy-start(bf16[128,5,64]{0,2,1:T(8,128)(2,1)S(1)} %pad_maximum_fusion.7) | copy-start | bytes 245764
  252.6 3.9 copy-start.32
  259.7 3.7 copy-start.21
  263.4 4.4 %copy-start.4 = (bf16[128,1024]{0,1:T(8,128)(2,1)S(1)}, bf16[128,1024]{0,1:T(8,128)(2,1)}, u32[]{:S(2)}) copy-start(bf16[128,1024]{0,1:T(8,128)(2,1)} %copy-done.3) | copy-start | bytes 786436
  263.4 4.4 %copy-start.19 = (bf16[128,2560]{1,0:T(8,128)(2,1)S(1)}, bf16[128,2560]{1,0:T(8,128)(2,1)}, u32[]{:S(2)}) copy-start(bf16[128,2560]{1,0:T(8,128)(2,1)} %copy-done.18) | copy-start | bytes 1966084
  267.9 3.9 copy-start.17
  271.7 3.8 copy-start.15
  271.7 3.8 copy-start.28
  279.3 143.4 %copy-start.10 = (f32[128,1024]{0,1:T(8,128)S(1)}, f32[128,1024]{0,1:T(8,128)}, u32[]{:S(2)}) copy-start(f32[128,1024]{0,1:T(8,128)} %copy-done.9) | copy-start | bytes 1572868
  279.3 143.4 %copy-start.13 = (f32[128,1024]{0,1:T(8,128)S(1)}, f32[128,1024]{0,1:T(8,128)}, u32[]{:S(2)}) copy-start(f32[128,1024]{0,1:T(8,128)} %copy-done.11) | copy-start | bytes 1572868
  279.3 143.4 %copy-start.36 = (f32[128,1024]{0,1:T(8,128)S(1)}, f32[128,1024]{0,1:T(8,128)}, u32[]{:S(2)}) copy-start(f32[128,1024]{0,1:T(8,128)} %get-tuple-element.600) | copy-start | bytes 1572868
  414.1 11.6 %copy-start.7 = (f32[128,1024]{0,1:T(8,128)S(1)}, f32[128,1024]{0,1:T(8,128)}, u32[]{:S(2)}) copy-start(f32[128,1024]{0,1:T(8,128)} %copy-done.6) | copy-start | bytes 1572868
  422.7 10.9 %copy-start.1 = (bf16[1,128,960]{1,2,0:T(8,128)(2,1)S(1)}, bf16[1,128,960]{1,2,0:T(8,128)(2,1)}, u32[]{:S(2)}) copy-start(bf16[1,128,960]{1,2,0:T(8,128)(2,1)} %param.16) | copy-start | bytes 737284
  425.7 6.2 %copy-start.30 = (f32[64,2560]{1,0:T(8,128)S(1)}, f32[64,2560]{1,0:T(8,128)}, u32[]{:S(2)}) copy-start(f32[64,2560]{1,0:T(8,128)} %get-tuple-element.416) | copy-start | bytes 1966084
  425.7 7.1 %copy-start.29 = (f32[64,2560]{1,0:T(8,128)S(1)}, f32[64,2560]{1,0:T(8,128)}, u32[]{:S(2)}) copy-start(f32[64,2560]{1,0:T(8,128)} %get-tuple-element.417) | copy-start | bytes 1966084

commit v2 on v1

--- a/solution.py
+++ b/solution.py
@@ -414,19 +414,19 @@
     first_shard = jnp.concatenate(
         [w_query, key_projection, value_projection, attn_gain[:, None], ffn_gain[:, None]], axis=1
     )
-    narrow_shards = [
-        jnp.pad(first_shard, rows_added),
+    narrow_shards = [jnp.pad(first_shard, rows_added)]
+    later_shards = [
         jnp.pad(jnp.transpose(w_out), rows_added),
         jnp.pad(jnp.transpose(w_down), rows_added),
     ]
     gate_shard, up_shard = jnp.pad(w_gate, rows_added), jnp.pad(w_up, rows_added)
     if reps % 2 == 0:
-        w_first, w_attn_out, w_d, w_both = ring_gather(
+        w_first, w_both = ring_gather(
             [*narrow_shards, jnp.stack([gate_shard, up_shard])], group, 0, True
         )
         w_g, w_u = w_both[0], w_both[1]
     else:
-        w_first, w_attn_out, w_d, w_g, w_u = ring_gather(
+        w_first, w_g, w_u = ring_gather(
             [*narrow_shards, gate_shard, up_shard], group, 0
         )
     qkv_width = query_width + 2 * key_width
@@ -447,7 +447,9 @@
         .astype(jnp.bfloat16)
         .reshape(row_count, key_width)
     )
-    every_key_row, every_value_row = ring_gather([key_row_block, value_rows], group, 1)
+    every_key_row, every_value_row, w_attn_out, w_d = ring_gather(
+        [key_row_block, value_rows, *later_shards], group, 1
+    )
     every_key_row = every_key_row.reshape(sequence_length, KEY_VALUE_HEADS, HEAD_WIDTH)
     every_value_row = every_value_row.reshape(sequence_length, KEY_VALUE_HEADS, HEAD_WIDTH)
     grouped_queries = query_row_block.reshape(row_count, KEY_VALUE_HEADS, group_ratio, HEAD_WIDTH)

time: 443 us -> 437 us (0.986)
  no operation moved by 1% of the time
where the time goes in v2:
time: 437 us; the launch traced here: 429 us
  Pallas kernels  314 us (72%)
  matrix products  56.3 us (13%)
  local copies, waits for them, and re-layouts  49.6 us (11%)
  other arithmetic  6.1 us (1%)
    pallas_call x2, Pallas kernels, ring_scatter(): pl.pallas_call(functools.partial(scatter_kernel, count, chips, reps), out...  193 us
    pallas_call x2, Pallas kernels, ring_gather(): pl.pallas_call(functools.partial(gather_kernel, count, chips, crossing),...  121 us
    slice x1, local copies, waits for them, and re-layouts, on_device(): w_g, w_u = (w_both[0], w_both[1])  9.17 us

profile of v2, /device:TPU:1, one launch (start us, length us, event | category | flops | bytes accessed | tf_op | source)
XLA Modules:
  0.0 428.7 jit_solution(13536685413435982921)
XLA Ops:
  1.6 1.3 multiply_reduce_fusion.5
  2.9 1.3 pad_bitcast_fusion
  4.2 0.9 pad_maximum_fusion.refs_1_
  6.2 65.5 %shard_map.203 = (bf16[16,64,1602]{2,1,0:T(8,128)(2,1)}, bf16[2,16,64,2560]{3,2,1,0:T(8,128)(2,1)}) custom-call(bf16[64,1602]{1,0:T(8,128)(2,1)} %pad.18.refs_0_, bf16[2,64,2560]{2,1,0:T(8,128)(2,1)} %pad_maximum_fusion.refs_1_), custom_call_target="tpu_custom_call" | custom-call | tf_op jit(solution)/shard_map/pallas_call | solution.py:214
  71.7 1.1 slice_convert_fusion
  73.1 3.5 fusion.65
  80.1 55.8 %shard_map.204 = (bf16[16,128,320]{2,1,0:T(8,128)(2,1)}, bf16[16,128,320]{2,1,0:T(8,128)(2,1)}, bf16[16,64,960]{2,1,0:T(8,128)(2,1)}, bf16[16,64,2560]{2,1,0:T(8,128)(2,1)}) custom-call(bf16[128,320]{1,0:T(8,128)(2,1)} %copy.135.refs_0_, bf16[128,320]{1,0:T(8,128)(2,1)} %copy.168.refs_1_, bf16[64,960]{1,0:T(8,128)(2,1)} %pad.21.refs_2_, ...), custom_call_target="tpu_custom_call" | custom-call | tf_op jit(solution)/shard_map/pallas_call | solution.py:214
  136.0 2.2 copy.136
  138.8 2.2 copy.137
  141.0 1.5 reshape_reshape.7
  142.5 1.1 slice.121
  144.0 4.8 %while.38 = (s32[]{:T(128)}, f32[5,3,128]{2,1,0:T(4,128)S(1)}, f32[5,3,128]{2,1,0:T(4,128)S(1)}, f32[5,3,128,64]{2,3,1,0:T(8,128)S(1)}, f32[5,3,128,64]{2,3,1,0:...) while((s32[]{:T(128)}, f32[5,3,128]{2,1,0:T(4,128)S(1)}, ...), condition=%wide.region_9.10_spmd.clone, body=%wide.region_5.9_spmd.clone.sunk | while | flops 398829440 | bytes 24654596 | solution.py:492
  145.1 0.9 fusion.186
  146.1 1.3 fusion.188
  147.4 1.2 fusion.187
  149.6 2.4 multiply_reduce_fusion.4
  152.3 9.2 %fusion.125 = (bf16[1,16,64,2560]{3,2,1,0:T(8,128)(2,1)}, bf16[1,16,64,2560]{3,2,1,0:T(8,128)(2,1)}) fusion(bf16[2,16,64,2560]{3,2,1,0:T(8,128)(2,1)} %get-tuple-element.404), kind=kLoop, calls=%fused_computation.189 | loop fusion | bytes 20971520 | tf_op jit(solution)/shard_map/slice | solution.py:427
  161.4 3.5 fusion.129
  166.7 1.3 fusion.78
  168.0 2.3 multiply_convert_fusion
  170.3 1.5 fusion.130
  171.8 1.7 multiply_reduce_fusion
  173.8 0.9 convolution_convert_fusion.5
  175.6 1.2 broadcast_in_dim.138.clone
  176.9 6.6 %while.39 = (s32[]{:T(128)}, f32[128,5,3,64]{0,3,2,1:T(8,128)S(1)}, bf16[2048,320]{0,1:T(8,128)(2,1)S(1)}, bf16[2048,320]{0,1:T(8,128)(2,1)}, s32[]{:T(128)}, /*...) while((s32[]{:T(128)}, f32[128,5,3,64]{0,3,2,1:T(8,128)S(1)}, ...), condition=%wide.region_15.16_spmd.clone, body=%wide.region_13.15_spmd.clone.sunk | while | flops 639752320 | bytes 23824664 | solution.py:594
  178.0 2.3 fusion.200
  183.6 1.6 copy.142
  185.3 1.6 copy.143
  186.8 58.2 %shard_map.205 = (f32[128,320]{1,0:T(8,128)}, f32[128,320]{1,0:T(8,128)}) custom-call(bf16[16,128,320]{2,1,0:T(8,128)(2,1)} %bitcast.251, bf16[16,128,320]{2,1,0:T(8,128)(2,1)} %bitcast.252), custom_call_target="tpu_custom_call" | custom-call | tf_op jit(solution)/shard_map/pallas_call | solution.py:361
  245.0 1.0 copy.144
  246.1 1.0 convert.54
  247.2 3.9 multiply_reduce_fusion.1
  251.3 0.9 copy.150.refs_5_
  252.2 2.2 convolution_convert_fusion.3
  254.4 3.6 copy.148
  258.0 1.8 convolution_convert_fusion.4
  259.8 2.7 copy.147
  262.5 3.9 convolution_convert_fusion
  266.4 3.9 convolution_convert_fusion.1
  270.3 3.8 convolution_convert_fusion.2
  274.0 134.7 %shard_map.206 = (f32[64,2560]{1,0:T(8,128)}, f32[64,2560]{1,0:T(8,128)}, f32[64,2560]{1,0:T(8,128)}, f32[64,960]{1,0:T(8,128)}, f32[64,1600]{1,0:T(8,128)}, /*index=5*/f32[64,2]{1,0:T(8,128)}) custom-call(bf16[16,64,2560]{2,1,0:T(8,128)(2,1)} %bitcast.244, bf16[16,64,2560]{2,1,0:T(8,128)(2,1)} %bitcast.243, bf16[16,64,2560]{2,1,0:T(8,128)(2,1)} %bitcast.242, ...), custom_call_target="tpu_custom_call" | custom-call | tf_op jit(solution)/shard_map/pallas_call | solution.py:361
  408.8 2.0 slice_bitcast_fusion
  410.8 1.7 slice.106
  412.5 1.7 slice_bitcast_fusion.1
  414.2 1.7 fusion.126
  415.9 1.5 slice_reduce_fusion
  417.4 2.9 fusion.81
  420.4 6.2 %fusion.88 = bf16[1,128,960]{1,2,0:T(8,128)(2,1)} fusion(s32[1024]{0:T(1024)S(1)} %fusion.118, pred[1024]{0:T(1024)(128)(4,1)S(1)} %fusion.119, f32[128,1024]{0,1:T(8,128)S(1)} %copy-done.7, bf16[128,2560]{1,0:T(8,128)(2,1)S(1)} %copy-done.28, bf16[1024,2560]{1,0:T(8,128)(2,1)} %bitcast.290), kind=kOutput, calls=%fused_computation.102 | convolution fusion | flops 925097984 | bytes 6673408 | tf_op jit(solution)/shard_map/td,wd->tw/dot_general | solution.py:517
  (165 shorter events, 17.7 us)
Async XLA Ops:
  0.6 1.0 copy-start
  0.7 4.5 %copy-start.38 = (bf16[60]{0:T(256)(128)(2,1)S(1)}, bf16[60]{0:T(256)(128)(2,1)}, u32[]{:S(2)}) copy-start(bf16[60]{0:T(256)(128)(2,1)} %param.19) | copy-start | bytes 364
  0.7 4.6 %copy-start.39 = (bf16[60]{0:T(256)(128)(2,1)S(1)}, bf16[60]{0:T(256)(128)(2,1)}, u32[]{:S(2)}) copy-start(bf16[60]{0:T(256)(128)(2,1)} %param.24) | copy-start | bytes 364
  0.7 4.7 %copy-start.35 = (bf16[60,960]{1,0:T(8,128)(2,1)S(1)}, bf16[60,960]{1,0:T(8,128)(2,1)}, u32[]{:S(2)}) copy-start(bf16[60,960]{1,0:T(8,128)(2,1)} %param.20) | copy-start | bytes 345604
  0.7 4.7 %copy-start.36 = (bf16[60,320]{1,0:T(8,128)(2,1)S(1)}, bf16[60,320]{1,0:T(8,128)(2,1)}, u32[]{:S(2)}) copy-start(bf16[60,320]{1,0:T(8,128)(2,1)} %param.21) | copy-start | bytes 115204
  0.7 4.7 %copy-start.37 = (bf16[60,320]{1,0:T(8,128)(2,1)S(1)}, bf16[60,320]{1,0:T(8,128)(2,1)}, u32[]{:S(2)}) copy-start(bf16[60,320]{1,0:T(8,128)(2,1)} %param.22) | copy-start | bytes 115204
  2.9 146.7 %copy-start.11 = (f32[128,1024]{0,1:T(8,128)}, f32[128,1024]{0,1:T(8,128)S(1)}, u32[]{:S(2)}) copy-start(f32[128,1024]{0,1:T(8,128)S(1)} %get-tuple-element.596) | copy-start | bytes 1572868
  5.5 71.2 %copy-start.40 = (s32[1,4]{1,0:T(1,128)S(1)}, s32[1,4]{1,0:T(1,128)}, u32[]{:S(2)}) copy-start(s32[1,4]{1,0:T(1,128)} %param.17) | copy-start | bytes 52
  71.7 7.0 %copy-start.31 = (bf16[2560,60]{0,1:T(8,128)(2,1)S(1)}, bf16[2560,60]{0,1:T(8,128)(2,1)}, u32[]{:S(2)}) copy-start(bf16[2560,60]{0,1:T(8,128)(2,1)} %param.27) | copy-start | bytes 921604
  72.9 6.6 %copy-start.34 = (bf16[960,60]{0,1:T(8,128)(2,1)S(1)}, bf16[960,60]{0,1:T(8,128)(2,1)}, u32[]{:S(2)}) copy-start(bf16[960,60]{0,1:T(8,128)(2,1)} %param.23) | copy-start | bytes 345604
  76.6 59.4 %copy-start.27 = (f32[128,1600]{0,1:T(8,128)}, f32[128,1600]{0,1:T(8,128)S(1)}, u32[]{:S(2)}) copy-start(f32[128,1600]{0,1:T(8,128)S(1)} %fusion.65) | copy-start | bytes 2457604
  144.3 1.8 copy-start.24
  148.8 0.8 copy-start.22
  149.6 2.4 copy-start.20
  152.0 21.5 %copy-start.6 = (f32[128,1024]{0,1:T(8,128)}, f32[128,1024]{0,1:T(8,128)S(1)}, u32[]{:S(2)}) copy-start(f32[128,1024]{0,1:T(8,128)S(1)} %get-tuple-element.598) | copy-start | bytes 1572868
  152.3 12.7 %copy-start.3 = (bf16[128,1024]{0,1:T(8,128)(2,1)}, bf16[128,1024]{0,1:T(8,128)(2,1)S(1)}, u32[]{:S(2)}) copy-start(bf16[128,1024]{0,1:T(8,128)(2,1)S(1)} %multiply_convert_fusion.3) | copy-start | bytes 786436
  161.4 4.0 copy-start.2
  161.4 6.5 %slice-start.2 = ((s8[5242880]{0:T(1024)(128)(4,1)}), s8[4194304]{0:T(1024)(128)(4,1)S(1)}, s32[]{:S(2)}) async-start(s8[5242880]{0:T(1024)(128)(4,1)} %bitcast.291), calls=%async_computation.2 | async-start | bytes 8388608
  165.0 1.7 copy-start.41
  165.5 2.5 slice-start.3
  166.7 5.2 %slice-start = ((s8[5242880]{0:T(1024)(128)(4,1)}), s8[4194304]{0:T(1024)(128)(4,1)S(1)}, s32[]{:S(2)}) async-start(s8[5242880]{0:T(1024)(128)(4,1)} %bitcast.238), calls=%async_computation | async-start | bytes 8388608
  168.0 5.6 %copy-start.14 = (f32[128,1024]{0,1:T(8,128)}, f32[128,1024]{0,1:T(8,128)S(1)}, u32[]{:S(2)}) copy-start(f32[128,1024]{0,1:T(8,128)S(1)} %fusion.78) | copy-start | bytes 1572868
  168.0 3.8 slice-start.1
  170.3 3.2 copy-start.16
  170.3 3.2 copy-start.18
  171.8 2.0 copy-start.5
  173.5 1.3 copy-start.23
  173.8 1.0 copy-start.9
  174.8 0.7 copy-start.25
  176.9 1.1 copy-start.26
  183.5 1.7 copy-start.8
  185.2 62.0 %copy-start.12 = (f32[128,1024]{0,1:T(8,128)S(1)}, f32[128,1024]{0,1:T(8,128)}, u32[]{:S(2)}) copy-start(f32[128,1024]{0,1:T(8,128)} %copy-done.11) | copy-start | bytes 1572868
  246.1 5.0 %copy-start.32 = (bf16[128,5,64]{0,2,1:T(8,128)(2,1)}, bf16[128,5,64]{0,2,1:T(8,128)(2,1)S(1)}, u32[]{:S(2)}) copy-start(bf16[128,5,64]{0,2,1:T(8,128)(2,1)S(1)} %pad_maximum_fusion.7) | copy-start | bytes 245764
  247.2 3.9 copy-start.33
  254.4 3.7 copy-start.21
  258.0 4.5 %copy-start.4 = (bf16[128,1024]{0,1:T(8,128)(2,1)S(1)}, bf16[128,1024]{0,1:T(8,128)(2,1)}, u32[]{:S(2)}) copy-start(bf16[128,1024]{0,1:T(8,128)(2,1)} %copy-done.3) | copy-start | bytes 786436
  258.0 4.5 %copy-start.19 = (bf16[128,2560]{1,0:T(8,128)(2,1)S(1)}, bf16[128,2560]{1,0:T(8,128)(2,1)}, u32[]{:S(2)}) copy-start(bf16[128,2560]{1,0:T(8,128)(2,1)} %copy-done.18) | copy-start | bytes 1966084
  262.5 3.9 copy-start.17
  266.4 3.9 copy-start.15
  266.4 3.9 copy-start.28
  274.0 143.4 %copy-start.10 = (f32[128,1024]{0,1:T(8,128)S(1)}, f32[128,1024]{0,1:T(8,128)}, u32[]{:S(2)}) copy-start(f32[128,1024]{0,1:T(8,128)} %copy-done.9) | copy-start | bytes 1572868
  274.0 143.4 %copy-start.13 = (f32[128,1024]{0,1:T(8,128)S(1)}, f32[128,1024]{0,1:T(8,128)}, u32[]{:S(2)}) copy-start(f32[128,1024]{0,1:T(8,128)} %copy-done.11) | copy-start | bytes 1572868
  274.0 143.4 %copy-start.42 = (f32[128,1024]{0,1:T(8,128)S(1)}, f32[128,1024]{0,1:T(8,128)}, u32[]{:S(2)}) copy-start(f32[128,1024]{0,1:T(8,128)} %get-tuple-element.600) | copy-start | bytes 1572868
  408.8 11.6 %copy-start.7 = (f32[128,1024]{0,1:T(8,128)S(1)}, f32[128,1024]{0,1:T(8,128)}, u32[]{:S(2)}) copy-start(f32[128,1024]{0,1:T(8,128)} %copy-done.6) | copy-start | bytes 1572868
  417.4 10.9 %copy-start.1 = (bf16[1,128,960]{1,2,0:T(8,128)(2,1)S(1)}, bf16[1,128,960]{1,2,0:T(8,128)(2,1)}, u32[]{:S(2)}) copy-start(bf16[1,128,960]{1,2,0:T(8,128)(2,1)} %param.16) | copy-start | bytes 737284
  420.4 6.2 %copy-start.30 = (f32[64,2560]{1,0:T(8,128)S(1)}, f32[64,2560]{1,0:T(8,128)}, u32[]{:S(2)}) copy-start(f32[64,2560]{1,0:T(8,128)} %get-tuple-element.416) | copy-start | bytes 1966084
  420.4 7.1 %copy-start.29 = (f32[64,2560]{1,0:T(8,128)S(1)}, f32[64,2560]{1,0:T(8,128)}, u32[]{:S(2)}) copy-start(f32[64,2560]{1,0:T(8,128)} %get-tuple-element.417) | copy-start | bytes 1966084
